TPU v7x, 32 devices: a whole 2x2x4 slice. The times are simulated.
32 devices in a mesh: section: 4 (over z), tp: 4 (over y, core), mirror: 2 (over x).
Axes of the slice: x: 2, y: 2, z: 4, core: 2. Of those that a mesh axis runs over, the one named last changes fastest.
Arguments:
- hidden: bfloat16 [2, 4, 2, 128, 14336], P(None, 'section', 'mirror', None, 'tp'), may hold values from -6 to 6
- incoming: bfloat16 [2, 4, 2, 128, 4096], P(None, 'section', 'mirror', None, 'tp'), may hold values from -0.3984375 to 0.3984375
- block_mask: int32 [2, 112, 32], P(None, 'tp'), may hold values from 0 to 1, as said below
Outputs:
- block_grads: bfloat16 [4, 4, 252, 128, 128], P('section', 'tp', 'mirror')
Inputs may be any that keep to these rules, and one draw needn't show every extreme that they name: `block_mask`: for every section and every index of tp, its 28 block rows keep between 7/16 and 9/16 of their blocks, at most 504; in every section exactly 504 on some index of tp.
All inputs are finite; a program needn't handle non-finite values.
Results may differ from a plain program's by a relative error of at most 0.006.
Values may be sent and summed in bfloat16 or wider, within the bound.
A program may use at most 128 MiB of HBM per device.

v0:
```python
import jax
import jax.numpy as jnp
from jax import lax
from jax.sharding import PartitionSpec as P

BLK = 128


def passed_along(block, axis, distance):
    devices = range(lax.axis_size(axis))
    route = [((i - distance) % len(devices), i) for i in devices]
    return lax.ppermute(block, axis, route)


def from_partner(value, axis, apart):
    mask = 2**apart
    pairs = [(source, source ^ mask) for source in range(lax.axis_size(axis))]
    return lax.ppermute(value, axis, pairs)


def group_of(slot_total):
    for size in range(min(slot_total, 28), 0, -1):
        return size
    return 1


def slot_table(mask_local, slot_total):
    flat = mask_local.reshape(-1)
    running = jnp.cumsum(flat)
    positions = jnp.arange(slot_total, dtype=jnp.int32)
    targets = jnp.sum((running[None, :] <= positions[:, None]).astype(jnp.int32), axis=1)
    usable = positions < running[-1]
    targets = jnp.minimum(targets, flat.shape[0] - 1)
    columns_count = mask_local.shape[1]
    return (targets // columns_count, targets % columns_count, usable)


def block_partials(hidden_rows, cotangent, block_rows, block_cols, usable, block_side):
    row_total = hidden_rows.shape[0]
    hidden_blocks = hidden_rows.reshape(row_total, -1, block_side)
    cot_blocks = cotangent.reshape(row_total, -1, block_side)
    slot_total = block_rows.shape[0]
    group_size = group_of(slot_total)

    def one_group(pieces):
        rows_piece, cols_piece, usable_piece = pieces
        left = jnp.take(hidden_blocks, rows_piece, axis=1)
        right = jnp.take(cot_blocks, cols_piece, axis=1)
        product = jnp.einsum("nkc,nkd->kcd", left, right, preferred_element_type=jnp.float32)
        product = jnp.where(usable_piece[:, None, None], product, 0.0)
        return product.astype(jnp.bfloat16)

    grouped = lax.map(
        one_group,
        (
            block_rows.reshape(-1, group_size),
            block_cols.reshape(-1, group_size),
            usable.reshape(-1, group_size),
        ),
    )
    return grouped.reshape(slot_total, block_side, block_side)


def body(hidden, incoming, block_mask):
    sections_total = lax.axis_size("section")
    half_count = sections_total // 2
    position = lax.axis_index("section")
    half_index = position // half_count
    section_index = position % half_count
    swap_bit = sections_total.bit_length() - 2
    block_side = BLK
    row_count = hidden.shape[3]
    down_part = passed_along(incoming[0, 0, 0], "section", -1)
    up_part = passed_along(incoming[1, 0, 0], "section", 1)
    arrived = jnp.stack([down_part, up_part])
    gathered = lax.all_gather(arrived, "tp", axis=2, tiled=True)
    cotangent = gathered.reshape(2 * row_count, gathered.shape[2])
    hidden_rows = hidden[:, 0, 0].reshape(2 * row_count, hidden.shape[4])
    mask_local = lax.dynamic_index_in_dim(block_mask, section_index, 0, keepdims=False)
    slot_total = mask_local.shape[0] * mask_local.shape[1] * 9 // 16
    slots_half = slot_total // 2
    block_rows, block_cols, usable = slot_table(mask_local, slot_total)
    partial_all = block_partials(hidden_rows, cotangent, block_rows, block_cols, usable, block_side)
    own_part = lax.dynamic_slice_in_dim(partial_all, half_index * slots_half, slots_half, 0)
    outgoing = lax.dynamic_slice_in_dim(partial_all, (1 - half_index) * slots_half, slots_half, 0)
    partner_part = from_partner(outgoing, "section", swap_bit)
    paired = (own_part.astype(jnp.float32) + partner_part.astype(jnp.float32)).astype(jnp.bfloat16)
    summed = lax.psum_scatter(
        paired.astype(jnp.float32).astype(jnp.bfloat16), "mirror", scatter_dimension=0, tiled=True
    )
    return summed.reshape(1, 1, -1, block_side, block_side)


def solution(mesh):
    placed = (
        P(None, "section", "mirror", None, "tp"),
        P(None, "section", "mirror", None, "tp"),
        P(None, "tp", None),
    )
    return jax.shard_map(
        body,
        mesh=mesh,
        in_specs=placed,
        out_specs=P("section", "tp", "mirror", None, None),
        check_vma=False,
    )
```

profile of v0, /device:TPU:0, one launch (start us, length us, event | category | flops | bytes accessed | tf_op | source)
XLA Modules:
  0.0 709.4 jit_solution(13503140052917762534)
XLA Ops:
  7.7 5.1 collective-permute-start
  12.8 6.7 collective-permute-done
  19.6 5.4 collective-permute-done.1
  32.6 15.4 %all-gather.2.cloned.1.call-done = bf16[2,128,4096]{2,1,0:T(8,128)(2,1)} async-done(((bf16[2,128,1024]{2,1,0:T(8,128)(2,1)}), bf16[2,128,4096]{2,1,0:T(8,128)(2,1)}) %all-gather.2.cloned.1.call-update) | async-done | bytes 2097168 | tf_op jit(solution)/shard_map/all_gather | solution.py:76
  52.2 173.5 %while.10 = (s32[]{:T(128)}, bf16[18,28,128,128]{3,2,1,0:T(8,128)(2,1)}, pred[18,28]{1,0:T(8,128)(4,1)S(1)}, s32[18,28]{1,0:T(8,128)S(1)}, bf16[256,28,128]{2,0,...) while((s32[]{:T(128)}, bf16[18,28,128,128]{3,2,1,0:T(8,128)(2,1)}, ...), condition=%wide.region_4.5_spmd, body=%wide.region_3.4_spmd.sunk | while | flops 237636096 | bytes 11937169 | solution.py:53
  57.9 3.9 fusion.34
  63.9 3.6 gather_fusion
  67.6 3.9 fusion.34
  73.6 3.6 gather_fusion
  77.2 3.9 fusion.34
  86.9 3.9 fusion.34
  92.9 3.6 gather_fusion
  96.5 3.9 fusion.34
  102.5 3.6 gather_fusion
  106.1 3.9 fusion.34
  112.1 3.6 gather_fusion
  115.8 3.9 fusion.34
  125.4 3.9 fusion.34
  135.1 3.9 fusion.34
  144.7 3.9 fusion.34
  154.4 3.9 fusion.34
  164.0 3.9 fusion.34
  173.6 3.9 fusion.34
  183.3 3.9 fusion.34
  192.9 4.0 fusion.34
  202.6 3.9 fusion.34
  212.2 3.9 fusion.34
  221.8 3.9 fusion.34
  225.8 10.2 %constant_dynamic-slice_fusion.2 = bf16[252,128,128]{2,1,0:T(8,128)(2,1)} fusion(bf16[504,128,128]{2,1,0:T(8,128)(2,1)} %bitcast.66, s32[]{:T(128)S(6)} %select_n.83), kind=kLoop, calls=%fused_computation.46 | loop fusion | bytes 16515076 | tf_op jit(solution)/shard_map/dynamic_slice | solution.py:85
  238.4 355.6 %collective-permute-done.2 = bf16[252,128,128]{2,1,0:T(8,128)(2,1)} collective-permute-done((bf16[252,128,128]{2,1,0:T(8,128)(2,1)}, bf16[252,128,128]{2,1,0:T(8,128)(2,1)}, u32[]{:S(2)}, u32[]{:S(2)}) %collective-permute-start.2) | collective-permute-done | bytes 8257568 | tf_op jit(solution)/shard_map/ppermute | solution.py:18
  594.0 10.7 %add_convert_fusion = bf16[252,128,128]{2,1,0:T(8,128)(2,1)} fusion(bf16[252,128,128]{2,1,0:T(8,128)(2,1)} %collective-permute-done.2, bf16[504,128,128]{2,1,0:T(8,128)(2,1)} %bitcast.67, s32[]{:T(128)S(6)} %select_n.82), kind=kLoop, calls=%fused_computation.27 | loop fusion | flops 16515072 | bytes 24772612 | tf_op jit(solution)/shard_map/convert_element_type | solution.py:87
  604.6 98.0 %reduce-scatter.2.cloned.1.call-done = bf16[126,128,128]{2,1,0:T(8,128)(2,1)} async-done(((bf16[252,128,128]{2,1,0:T(8,128)(2,1)}), bf16[126,128,128]{2,1,0:T(8,128)(2,1)}) %reduce-scatter.2.cloned.1.call-update) | async-done | bytes 4128784 | tf_op jit(solution)/shard_map/reduce_scatter | solution.py:88
  (151 shorter events, 99.9 us)
Async XLA Ops:
  6.5 19.4 %copy-start = (s32[2,28,32]{2,0,1:T(2,128)S(1)}, s32[2,28,32]{2,0,1:T(2,128)}, u32[]{:S(2)}) copy-start(s32[2,28,32]{2,0,1:T(2,128)} %param.7) | copy-start | bytes 21508
  6.5 21.1 %copy-start.1 = (bf16[2,1,1,128,3584]{4,3,2,1,0:T(8,128)(2,1)S(1)}, bf16[2,1,1,128,3584]{4,3,2,1,0:T(8,128)(2,1)}, u32[]{:S(2)}) copy-start(bf16[2,1,1,128,3584]{4,3,2,1,0:T(8,128)(2,1)} %param.5) | copy-start | bytes 5505028
  6.5 41.5 %all-gather.2.cloned.1.call-start = ((), (), s32[]{:S(2)}) async-start(), calls=%async_computation.1 | async-start | bytes 2621440 | tf_op jit(solution)/shard_map/all_gather | solution.py:76
  7.7 11.8 %collective-permute-start = (bf16[128,1024]{1,0:T(8,128)(2,1)S(1)}, bf16[128,1024]{1,0:T(8,128)(2,1)S(1)}, u32[]{:S(2)}, u32[]{:S(2)}) collective-permute-start(bf16[128,1024]{1,0:T(8,128)(2,1)S(1)} %get-tuple-element.82), channel_id=1, source_target_pairs={{8,0},{16,8},{24,16},{0,24},{9,1},{17,9},{25,17},{1,25},{10,2},{18... | collective-permute-start | bytes 786440 | tf_op jit(solution)/shard_map/ppermute | solution.py:12
  12.8 12.1 %collective-permute-start.1 = (bf16[128,1024]{1,0:T(8,128)(2,1)S(1)}, bf16[128,1024]{1,0:T(8,128)(2,1)S(1)}, u32[]{:S(2)}, u32[]{:S(2)}) collective-permute-start(bf16[128,1024]{1,0:T(8,128)(2,1)S(1)} %get-tuple-element.83), channel_id=1, source_target_pairs={{24,0},{0,8},{8,16},{16,24},{25,1},{1,9},{9,17},{17,25},{26,2},{2,... | collective-permute-start | bytes 786440 | tf_op jit(solution)/shard_map/ppermute | solution.py:12
  25.8 676.8 %reduce-scatter.2.cloned.1.call-start = ((), (), s32[]{:S(2)}) async-start(), calls=%async_computation.2 | async-start | bytes 12386304 | tf_op jit(solution)/shard_map/reduce_scatter | solution.py:88
  236.0 358.0 %collective-permute-start.2 = (bf16[252,128,128]{2,1,0:T(8,128)(2,1)}, bf16[252,128,128]{2,1,0:T(8,128)(2,1)}, u32[]{:S(2)}, u32[]{:S(2)}) collective-permute-start(bf16[252,128,128]{2,1,0:T(8,128)(2,1)} %constant_dynamic-slice_fusion.2), channel_id=1, source_target_pairs={{0,16},{8,24},{16,0},{24,8},{1,17},{9,25},{17,1},{25,9},{2,18},{10... | collective-permute-start | bytes 24772616 | tf_op jit(solution)/shard_map/ppermute | solution.py:18
Sparse Core Ops, SparseCore 0:
  25.9 22.0 all-gather.1
  604.8 97.7 reduce-scatter.1
where the time goes:
time: 710 us; the launch traced here: 709 us
  waiting for transfers between devices  481 us (68%)
  local copies, waits for them, and re-layouts  123 us (17%)
  matrix products  70.2 us (10%)
  other arithmetic  13.5 us (2%)
  between operations  13.5 us (2%)
  starting transfers between devices  7.56 us (1%)
    ppermute x1, waiting for transfers between devices, from_partner(): return lax.ppermute(value, axis, pairs)  356 us
    reduce_scatter x1, waiting for transfers between devices, body(): lax.psum_scatter(paired.astype(jnp.float32).astype(jnp.bfloat16), 'mirror...  98 us
    dot_general x18, matrix products, one_group(): jnp.einsum('nkc,nkd->kcd', left, right, preferred_element_type=jnp.float32)  70.2 us
    gather x18, local copies, waits for them, and re-layouts, one_group(): right = jnp.take(cot_blocks, cols_piece, axis=1)  65.4 us
    gather x18, local copies, waits for them, and re-layouts, one_group(): left = jnp.take(hidden_blocks, rows_piece, axis=1)  36.4 us
    all_gather x1, waiting for transfers between devices, body(): gathered = lax.all_gather(arrived, 'tp', axis=2, tiled=True)  15.4 us
  transfers between devices with their start and end apart: 5, of which 5 were waited for; matrix products, arithmetic and copies ran while one was open for 1% of the time, Pallas kernels for 0%

commit v1 on v0

v1 whole, which is shorter than its diff:
```python
import functools

import jax
import jax.numpy as jnp
from jax import lax
from jax.experimental import pallas as pl
from jax.experimental.pallas import tpu as pltpu
from jax.sharding import PartitionSpec as P

BLK = 128
MESH = pl.DeviceIdType.MESH


def cdiv(a, b):
    return -(-a // b)


def windows(rows, cols):
    kept_min, cap = rows * cols * 7 // 16, rows * cols * 9 // 16

    def span(first, last):
        return first // cols, min(rows - 1, rows - max(1, cdiv(kept_min - last, cols)))

    halves = [span(h * cap // 2, (h + 1) * cap // 2 - 1) for h in range(2)]
    quarters = [span(q * cap // 4, (q + 1) * cap // 4 - 1) for q in range(4)]
    hw = max(b - a + 1 for a, b in halves)
    qw = max(b - a + 1 for a, b in quarters)
    hs = [min(a, rows - hw) for a, _ in halves]
    qs = [min(a, rows - qw) for a, _ in quarters]
    for q in range(4):
        h = q // 2
        qs[q] = max(hs[h], min(qs[q], hs[h] + hw - qw))
        assert qs[q] <= quarters[q][0] and qs[q] + qw > quarters[q][1]
        assert hs[h] <= halves[h][0] and hs[h] + hw > halves[h][1]
    return hw, qw, hs, qs


def pick(table, half, m):
    return (1 - half) * ((1 - m) * table[0] + m * table[1]) + half * ((1 - m) * table[2] + m * table[3])


def flip(u, bit):
    return u + bit * (1 - 2 * ((u // bit) % 2))


def flips(u, mask, top):
    bit = 1
    while bit < top:
        if mask & bit:
            u = flip(u, bit)
        bit *= 2
    return u


def kernel(sizes, rel_ref, col_ref, use_ref, h_ref, inc_ref, out_ref,
           inc_b, c00, c01, c10, c11, zh, xh0, xh1, h_t, acc,
           zc_s, zc_r, zh_s, zh_r, xo_s, xo_r, xr_s, xr_r, xc_s, xc_r, tc_s, tc_r):
    S, T, rows, hw, qw, hs, qs, slots, nch, unroll, cpt = sizes
    p, t, m = lax.axis_index("section"), lax.axis_index("tp"), lax.axis_index("mirror")
    half = p // (S // 2)
    other = 1 - m
    hstart = (1 - half) * hs[0] + half * hs[1]
    hstart_there = half * hs[0] + (1 - half) * hs[1]
    qstart = pick(qs, half, m)
    qstart_there = pick(qs, half, other)
    partner = (p + S // 2) % S
    C = ((c00, c01), (c10, c11))

    def cols(start, n):
        return pl.ds(pl.multiple_of(start * BLK, BLK), n * BLK)

    mine = pl.ds(t * cpt, cpt)

    offsets = sorted({(sgn + s * (S // 2)) % S for sgn in (1, -1) for s in (0, 1)} | {S // 2})
    bits = []
    b = T // 2
    while b >= 1:
        bits.append(b)
        b //= 2
    peers = [{"section": (p + o) % S} for o in offsets] + [{"mirror": other}] + [{"tp": flip(t, b)} for b in bits]
    barrier = pltpu.get_barrier_semaphore()
    for peer in peers:
        pl.semaphore_signal(barrier, inc=1, device_id=peer, device_id_type=MESH)
    for d in range(2):
        for c in range(cpt):
            inc_b[d, c] = inc_ref[d, :, c * BLK:(c + 1) * BLK]
    pl.semaphore_wait(barrier, len(peers))

    def copy(src, dst, ss, rs, dev):
        return pltpu.make_async_remote_copy(
            src_ref=src, dst_ref=dst, send_sem=ss, recv_sem=rs, device_id=dev, device_id_type=MESH)

    zc = {}
    for s in range(2):
        for d in range(2):
            i = 2 * s + d
            dest = (p + (S - 1 if d == 0 else 1) + s * (S // 2)) % S
            zc[s, d] = copy(inc_b.at[d], C[s][0].at[d, mine], zc_s.at[i], zc_r.at[i], {"section": dest})
    per = nch // 2
    step = rows // per
    zhc, xr = [], []
    for i in range(nch):
        d, r = i // per, pl.ds((i % per) * step, step)
        zhc.append(copy(h_ref.at[d, r, cols(hstart_there, hw)], zh.at[d, r], zh_s.at[i], zh_r.at[i],
                        {"section": partner}))
        xr.append(copy(zh.at[d, r, cols(qstart_there - hstart, qw)], xh1.at[d, r], xr_s.at[i], xr_r.at[i],
                       {"mirror": other}))
    xo = [copy(h_ref.at[d, :, cols(qstart_there, qw)], xh0.at[d], xo_s.at[d], xo_r.at[d], {"mirror": other})
          for d in range(2)]
    xc = {}
    for s in range(2):
        for d in range(2):
            i = 2 * s + d
            xc[s, d] = copy(C[s][0].at[d, mine], C[s][1].at[d, mine], xc_s.at[i], xc_r.at[i], {"mirror": other})
    tc = {}
    stage_rels = []
    have = [0]
    for k, b in enumerate(bits):
        stage_rels.append(list(have))
        have = have + [r | b for r in have]
    for s in range(2):
        for d in range(2):
            for mr in range(2):
                n = ((s * 2 + d) * 2 + mr) * (T - 1)
                for k, b in enumerate(bits):
                    for r in stage_rels[k]:
                        u = flips(t, r, T)
                        ref = C[s][mr].at[d, pl.ds(u * cpt, cpt)]
                        tc[s, d, mr, k, r] = copy(ref, ref, tc_s.at[n], tc_r.at[n], {"tp": flip(t, b)})
                        n += 1

    def spread(s, d, mr, r, after):
        for k in range(after + 1, len(bits)):
            tc[s, d, mr, k, r].start()

    def stage_wait(s, mr, k):
        for d in range(2):
            for r in stage_rels[k]:
                tc[s, d, mr, k, r].wait_recv()
                spread(s, d, mr, r | bits[k], k)

    def relay(i):
        zhc[i].wait_recv()
        xr[i].start()
        zhc[i].wait_send()
        if i + 2 < nch:
            zhc[i + 2].start()

    def compute(s, mr, src, first, kind):
        def turn(b, carry):
            blk = src[:, :, cols(first + b, 1)].reshape(2 * rows, BLK)
            h_t[b] = blk.T
            return carry

        lax.fori_loop(0, qw, turn, 0)
        cot = C[s][mr]

        def group(g, carry):
            for e in range(unroll):
                k = g * unroll + e
                right = cot[:, col_ref[k]].reshape(2 * rows, BLK)
                got = jnp.dot(h_t[rel_ref[k]], right, preferred_element_type=jnp.float32)
                if kind != "first":
                    got = got + acc[k]
                if kind == "last":
                    out_ref[k] = (got * use_ref[k]).astype(out_ref.dtype)
                else:
                    acc[k] = got
            return carry

        lax.fori_loop(0, slots // unroll, group, 0)

    for d in range(2):
        for s in range(2):
            zc[s, d].start()
    for c in xo:
        c.start()
    zhc[0].start()
    zhc[1].start()
    for s in range(2):
        for d in range(2):
            zc[s, d].wait_recv()
            xc[s, d].start()
            spread(s, d, 0, 0, -1)
    for s in range(2):
        for d in range(2):
            xc[s, d].wait_recv()
            spread(s, d, 1, 0, -1)
    relay(0)
    relay(1)
    for k in range(len(bits)):
        stage_wait(0, 0, k)
    compute(0, 0, h_ref, qstart, "first")
    relay(2)
    for k in range(len(bits)):
        stage_wait(0, 1, k)
    for c in xo:
        c.wait_recv()
    relay(3)
    compute(0, 1, xh0, 0, "add")
    for i in range(4, nch):
        relay(i)
    for mr in range(2):
        for k in range(len(bits)):
            stage_wait(1, mr, k)
    compute(1, 0, zh, qstart - hstart, "add")
    for c in xr:
        c.wait_recv()
    compute(1, 1, xh1, 0, "last")
    for c in list(zc.values()) + xo + list(xc.values()) + list(tc.values()) + xr:
        c.wait_send()


def body(hidden, incoming, block_mask):
    S, T = lax.axis_size("section"), lax.axis_size("tp")
    p, m = lax.axis_index("section"), lax.axis_index("mirror")
    _, ffb, db = block_mask.shape
    rows, ff, dm = hidden.shape[3], hidden.shape[4], incoming.shape[4]
    cap = ffb * db * 9 // 16
    slots = cap // 4
    hw, qw, hs, qs = windows(ffb, db)
    half = p // (S // 2)
    mask = lax.dynamic_index_in_dim(block_mask, p % (S // 2), 0, keepdims=False)
    running = jnp.cumsum(mask.reshape(-1))
    positions = (2 * half + m) * slots + jnp.arange(slots, dtype=jnp.int32)
    targets = jnp.sum((running[None, :] <= positions[:, None]).astype(jnp.int32), axis=1)
    use = (positions < running[-1]).astype(jnp.float32)
    targets = jnp.minimum(targets, ffb * db - 1)
    rel = jnp.clip(targets // db - pick(qs, half, m), 0, qw - 1)
    col = targets % db
    per_t = dm // BLK
    nch = 8
    unroll = max(u for u in range(1, 10) if slots % u == 0)
    sizes = (S, T, rows, hw, qw, hs, qs, slots, nch, unroll, per_t)
    bf = jnp.bfloat16
    vmem, smem = pl.BlockSpec(memory_space=pltpu.VMEM), pl.BlockSpec(memory_space=pltpu.SMEM)
    dma = pltpu.SemaphoreType.DMA
    n_tc = 8 * (T - 1)
    out = pl.pallas_call(
        functools.partial(kernel, sizes),
        out_shape=jax.ShapeDtypeStruct((slots, BLK, BLK), bf),
        in_specs=[smem] * 3 + [vmem] * 2,
        out_specs=vmem,
        scratch_shapes=[pltpu.VMEM((2, per_t, rows, BLK), bf)] + [pltpu.VMEM((2, db, rows, BLK), bf)] * 4
        + [pltpu.VMEM((2, rows, hw * BLK), bf)]
        + [pltpu.VMEM((2, rows, qw * BLK), bf)] * 2
        + [pltpu.VMEM((qw, BLK, 2 * rows), bf), pltpu.VMEM((slots, BLK, BLK), jnp.float32)]
        + [dma((4,)), dma((4,)), dma((nch,)), dma((nch,)), dma((2,)), dma((2,)), dma((nch,)), dma((nch,)),
           dma((4,)), dma((4,)), dma((n_tc,)), dma((n_tc,))],
        compiler_params=pltpu.CompilerParams(
            collective_id=0, has_side_effects=True, vmem_limit_bytes=48 * 1024 * 1024),
        cost_estimate=pl.CostEstimate(
            flops=slots * BLK * BLK * rows * 16, bytes_accessed=8 * 1024 * 1024, transcendentals=0),
    )(rel.astype(jnp.int32), col.astype(jnp.int32), use,
      hidden.reshape(2, rows, ff), incoming.reshape(2, rows, dm))
    return out.reshape(1, 1, slots, BLK, BLK)


def solution(mesh):
    placed = (
        P(None, "section", "mirror", None, "tp"),
        P(None, "section", "mirror", None, "tp"),
        P(None, "tp", None),
    )
    return jax.shard_map(
        body,
        mesh=mesh,
        in_specs=placed,
        out_specs=P("section", "tp", "mirror", None, None),
        check_vma=False,
    )
```

time: 710 us -> 139 us (0.20)
  waiting for transfers between devices: 481 us -> 0 us
  Pallas kernels: 0 us -> 128 us
  local copies, waits for them, and re-layouts: 123 us -> 8.91 us
  matrix products: 70.2 us -> 0 us
  between operations: 13.5 us -> 0.04 us
  other arithmetic: 13.5 us -> 1.25 us
  starting transfers between devices: 7.56 us -> 0 us
    ppermute x3 -> x0, waiting for transfers between devices: 368 us -> none  [the longest x1 356 us: from_partner(): return lax.ppermute(value, axis, pairs)]
    pallas_call x0 -> x1, Pallas kernels: none -> 128 us  [body(): pl.pallas_call(functools.partial(kernel, sizes), out_shape=jax.ShapeDtype...]
    gather x36 -> x0, local copies, waits for them, and re-layouts: 102 us -> none  [the longest x18 65.4 us: one_group(): right = jnp.take(cot_blocks, cols_piece, axis=1)]
    reduce_scatter x1 -> x0, waiting for transfers between devices: 98 us -> none  [body(): lax.psum_scatter(paired.astype(jnp.float32).astype(jnp.bfloat16), 'mirror...]
    dot_general x18 -> x0, matrix products: 70.2 us -> none  [one_group(): jnp.einsum('nkc,nkd->kcd', left, right, preferred_element_type=jnp.float32)]
    all_gather x1 -> x0, waiting for transfers between devices: 15.4 us -> none  [body(): gathered = lax.all_gather(arrived, 'tp', axis=2, tiled=True)]
    dynamic_slice x2 -> x1, local copies, waits for them, and re-layouts: 10.3 us -> 0.05 us  [body(): mask = lax.dynamic_index_in_dim(block_mask, p % (S // 2), 0, keepdims=False)]
    convert_element_type x1, other arithmetic: 10.7 us -> 0.66 us  [body(): use = (positions < running[-1]).astype(jnp.float32)]
  transfers between devices with their start and end apart: 5 -> 0, of which waited for: 5 -> 0; matrix products, arithmetic and copies ran while one was open for 1% -> 0% of each run, Pallas kernels for 0% -> 0%
where the time goes in v1:
time: 139 us
  Pallas kernels  128 us (92%)
  local copies, waits for them, and re-layouts  8.91 us (6%)
    pallas_call x1, Pallas kernels, body(): pl.pallas_call(functools.partial(kernel, sizes), out_shape=jax.ShapeDtype...  128 us
    unnamed x7, local copies, waits for them, and re-layouts  8.01 us

profile of v1, /device:TPU:0, one launch (start us, length us, event | category | flops | bytes accessed | tf_op | source)
XLA Modules:
  0.0 138.7 jit_solution(17327700657867921055)
XLA Ops:
  0.0 0.0 copy-start
  0.0 0.7 copy-done
  0.7 0.1 dynamic-slice_reduce_fusion
  0.8 0.1 reshape.42
  0.9 0.3 reduce-window.9
  1.2 0.1 slice.10
  1.3 0.1 slice_reduce_fusion
  1.4 0.1 add_bitcast_fusion
  1.5 0.6 slice.12
  2.0 0.2 convert_reduce_fusion
  2.2 0.7 compare_convert_fusion.use_ref
  2.9 0.0 copy-start.1
  2.9 1.5 %copy-done.1 = bf16[2,1,1,128,3584]{4,3,2,1,0:T(8,128)(2,1)S(1)} copy-done((bf16[2,1,1,128,3584]{4,3,2,1,0:T(8,128)(2,1)S(1)}, bf16[2,1,1,128,3584]{4,3,2,1,0:T(8,128)(2,1)}, u32[]{:S(2)}) %copy-start.1) | copy-done | bytes 1835032
  4.4 0.0 copy-start.2
  4.4 1.0 copy-done.2
  5.5 128.5 %shard_map.37 = bf16[126,128,128]{2,1,0:T(8,128)(2,1)} custom-call(s32[126]{0:T(128)S(1)} %get-tuple-element.6.rel_ref, s32[126]{0:T(128)S(1)} %get-tuple-element.5.col_ref, f32[126]{0:T(128)S(1)} %compare_convert_fusion.use_ref, bf16[2,128,3584]{2,1,0:T(8,128)(2,1)S(1)} %bitcast.6, bf16[2,128,1024]{2,1,0:T(8,128)(2,1)S(1)} %bitcast.7), custom_call_target="tpu_custom_call" | custom-call | flops 4227858432 | bytes 8388608 | tf_op jit(solution)/shard_map/pallas_call | solution.py:239
  133.9 4.7 %copy.5 = bf16[1,1,126,128,128]{4,3,2,1,0:T(8,128)(2,1)} copy(bf16[1,1,126,128,128]{4,3,2,1,0:T(8,128)(2,1)} %bitcast.8) | data formatting | bytes 8257536
  (3 shorter events, 0.0 us)
Async XLA Ops:
  0.0 0.7 copy-start
  2.9 1.5 %copy-start.1 = (bf16[2,1,1,128,3584]{4,3,2,1,0:T(8,128)(2,1)S(1)}, bf16[2,1,1,128,3584]{4,3,2,1,0:T(8,128)(2,1)}, u32[]{:S(2)}) copy-start(bf16[2,1,1,128,3584]{4,3,2,1,0:T(8,128)(2,1)} %param.3) | copy-start | bytes 5505028
  4.4 1.0 copy-start.2

commit v2 on v1

--- a/solution.py
+++ b/solution.py
@@ -53,7 +53,7 @@
 
 
 def kernel(sizes, rel_ref, col_ref, use_ref, h_ref, inc_ref, out_ref,
-           inc_b, c00, c01, c10, c11, zh, xh0, xh1, h_t, acc,
+           inc_b, c00, c01, c10, c11, zh, xh0, xh1, h_t, acc, inc_v, own, in_s,
            zc_s, zc_r, zh_s, zh_r, xo_s, xo_r, xr_s, xr_r, xc_s, xc_r, tc_s, tc_r):
     S, T, rows, hw, qw, hs, qs, slots, nch, unroll, cpt = sizes
     p, t, m = lax.axis_index("section"), lax.axis_index("tp"), lax.axis_index("mirror")
@@ -81,9 +81,14 @@
     barrier = pltpu.get_barrier_semaphore()
     for peer in peers:
         pl.semaphore_signal(barrier, inc=1, device_id=peer, device_id_type=MESH)
+    fetch_inc = pltpu.make_async_copy(inc_ref, inc_v, in_s.at[0])
+    fetch_own = pltpu.make_async_copy(h_ref.at[:, :, cols(qstart, qw)], own, in_s.at[1])
+    fetch_inc.start()
+    fetch_own.start()
+    fetch_inc.wait()
     for d in range(2):
         for c in range(cpt):
-            inc_b[d, c] = inc_ref[d, :, c * BLK:(c + 1) * BLK]
+            inc_b[d, c] = inc_v[d, :, c * BLK:(c + 1) * BLK]
     pl.semaphore_wait(barrier, len(peers))
 
     def copy(src, dst, ss, rs, dev):
@@ -139,26 +144,27 @@
                 tc[s, d, mr, k, r].wait_recv()
                 spread(s, d, mr, r | bits[k], k)
 
+    ahead = 4
+
     def relay(i):
         zhc[i].wait_recv()
         xr[i].start()
         zhc[i].wait_send()
-        if i + 2 < nch:
-            zhc[i + 2].start()
-
-    def compute(s, mr, src, first, kind):
+        if i + ahead < nch:
+            zhc[i + ahead].start()
+
+    def compute(lefts, rights, kind):
         def turn(b, carry):
-            blk = src[:, :, cols(first + b, 1)].reshape(2 * rows, BLK)
+            blk = jnp.concatenate([ref[d, :, cols(first + b, 1)] for ref, d, first in lefts], axis=0)
             h_t[b] = blk.T
             return carry
 
         lax.fori_loop(0, qw, turn, 0)
-        cot = C[s][mr]
 
         def group(g, carry):
             for e in range(unroll):
                 k = g * unroll + e
-                right = cot[:, col_ref[k]].reshape(2 * rows, BLK)
+                right = jnp.concatenate([ref[d, col_ref[k]] for ref, d in rights], axis=0)
                 got = jnp.dot(h_t[rel_ref[k]], right, preferred_element_type=jnp.float32)
                 if kind != "first":
                     got = got + acc[k]
@@ -182,31 +188,41 @@
             zc[s, d].wait_recv()
             xc[s, d].start()
             spread(s, d, 0, 0, -1)
+    zhc[2].start()
+    zhc[3].start()
     for s in range(2):
         for d in range(2):
             xc[s, d].wait_recv()
             spread(s, d, 1, 0, -1)
     relay(0)
     relay(1)
-    for k in range(len(bits)):
-        stage_wait(0, 0, k)
-    compute(0, 0, h_ref, qstart, "first")
     relay(2)
-    for k in range(len(bits)):
-        stage_wait(0, 1, k)
+    for k in range(len(bits) - 1):
+        for mr in range(2):
+            stage_wait(0, mr, k)
+    relay(3)
+    last = len(bits) - 1
+    stage_wait(0, 0, last)
+    fetch_own.wait()
+    compute([(own, 0, 0), (own, 1, 0)], [(c00, 0), (c00, 1)], "first")
+    relay(4)
+    stage_wait(0, 1, last)
     for c in xo:
         c.wait_recv()
-    relay(3)
-    compute(0, 1, xh0, 0, "add")
-    for i in range(4, nch):
-        relay(i)
-    for mr in range(2):
-        for k in range(len(bits)):
+    compute([(xh0, 0, 0), (xh0, 1, 0)], [(c01, 0), (c01, 1)], "add")
+    relay(5)
+    for k in range(len(bits)):
+        for mr in range(2):
             stage_wait(1, mr, k)
-    compute(1, 0, zh, qstart - hstart, "add")
-    for c in xr:
+    for c in xr[:per]:
         c.wait_recv()
-    compute(1, 1, xh1, 0, "last")
+    mid = qstart - hstart
+    compute([(zh, 0, mid), (xh1, 0, 0)], [(c10, 0), (c11, 0)], "add")
+    relay(6)
+    relay(7)
+    for c in xr[per:]:
+        c.wait_recv()
+    compute([(zh, 1, mid), (xh1, 1, 0)], [(c10, 1), (c11, 1)], "last")
     for c in list(zc.values()) + xo + list(xc.values()) + list(tc.values()) + xr:
         c.wait_send()
 
@@ -234,17 +250,19 @@
     sizes = (S, T, rows, hw, qw, hs, qs, slots, nch, unroll, per_t)
     bf = jnp.bfloat16
     vmem, smem = pl.BlockSpec(memory_space=pltpu.VMEM), pl.BlockSpec(memory_space=pltpu.SMEM)
+    hbm = pl.BlockSpec(memory_space=pltpu.HBM)
     dma = pltpu.SemaphoreType.DMA
     n_tc = 8 * (T - 1)
     out = pl.pallas_call(
         functools.partial(kernel, sizes),
         out_shape=jax.ShapeDtypeStruct((slots, BLK, BLK), bf),
-        in_specs=[smem] * 3 + [vmem] * 2,
+        in_specs=[smem] * 3 + [hbm] * 2,
         out_specs=vmem,
         scratch_shapes=[pltpu.VMEM((2, per_t, rows, BLK), bf)] + [pltpu.VMEM((2, db, rows, BLK), bf)] * 4
         + [pltpu.VMEM((2, rows, hw * BLK), bf)]
         + [pltpu.VMEM((2, rows, qw * BLK), bf)] * 2
         + [pltpu.VMEM((qw, BLK, 2 * rows), bf), pltpu.VMEM((slots, BLK, BLK), jnp.float32)]
+        + [pltpu.VMEM((2, rows, dm), bf), pltpu.VMEM((2, rows, qw * BLK), bf), dma((2,))]
         + [dma((4,)), dma((4,)), dma((nch,)), dma((nch,)), dma((2,)), dma((2,)), dma((nch,)), dma((nch,)),
            dma((4,)), dma((4,)), dma((n_tc,)), dma((n_tc,))],
         compiler_params=pltpu.CompilerParams(

time: 139 us -> 126 us (0.906); the launches traced: 139 us -> 124 us
  Pallas kernels: 128 us -> 114 us
    pallas_call x1, Pallas kernels: 128 us -> 114 us  [body(): pl.pallas_call(functools.partial(kernel, sizes), out_shape=jax.ShapeDtype...]
where the time goes in v2:
time: 126 us; the launch traced here: 124 us
  Pallas kernels  114 us (90%)
  local copies, waits for them, and re-layouts  8.91 us (7%)
    pallas_call x1, Pallas kernels, body(): pl.pallas_call(functools.partial(kernel, sizes), out_shape=jax.ShapeDtype...  114 us
    unnamed x7, local copies, waits for them, and re-layouts  8.01 us

profile of v2, /device:TPU:0, one launch (start us, length us, event | category | flops | bytes accessed | tf_op | source)
XLA Modules:
  0.0 124.3 jit_solution(4960708876087296291)
XLA Ops:
  0.0 0.0 copy-start
  0.0 0.7 copy-done
  0.7 0.1 dynamic-slice_reduce_fusion
  0.8 0.1 reshape.42
  0.9 0.3 reduce-window.9
  1.2 0.1 slice.10
  1.3 0.1 slice_reduce_fusion
  1.4 0.1 add_bitcast_fusion
  1.5 0.6 slice.12
  2.0 0.2 convert_reduce_fusion
  2.2 0.7 compare_convert_fusion.use_ref
  2.9 0.0 copy-start.1
  2.9 1.5 %copy-done.1 = bf16[2,1,1,128,3584]{4,3,2,1,0:T(8,128)(2,1)S(1)} copy-done((bf16[2,1,1,128,3584]{4,3,2,1,0:T(8,128)(2,1)S(1)}, bf16[2,1,1,128,3584]{4,3,2,1,0:T(8,128)(2,1)}, u32[]{:S(2)}) %copy-start.1) | copy-done | bytes 1835032
  4.4 0.0 copy-start.2
  4.4 1.0 copy-done.2
  5.5 114.1 %shard_map.37 = bf16[126,128,128]{2,1,0:T(8,128)(2,1)} custom-call(s32[126]{0:T(128)S(1)} %get-tuple-element.6.rel_ref, s32[126]{0:T(128)S(1)} %get-tuple-element.5.col_ref, f32[126]{0:T(128)S(1)} %compare_convert_fusion.use_ref, bf16[2,128,3584]{2,1,0:T(8,128)(2,1)S(1)} %bitcast.6, bf16[2,128,1024]{2,1,0:T(8,128)(2,1)S(1)} %bitcast.7), custom_call_target="tpu_custom_call" | custom-call | flops 4227858432 | bytes 8388608 | tf_op jit(solution)/shard_map/pallas_call | solution.py:256
  119.5 4.7 %copy.5 = bf16[1,1,126,128,128]{4,3,2,1,0:T(8,128)(2,1)} copy(bf16[1,1,126,128,128]{4,3,2,1,0:T(8,128)(2,1)} %bitcast.8) | data formatting | bytes 8257536
  (3 shorter events, 0.0 us)
Async XLA Ops:
  0.0 0.7 copy-start
  2.9 1.5 %copy-start.1 = (bf16[2,1,1,128,3584]{4,3,2,1,0:T(8,128)(2,1)S(1)}, bf16[2,1,1,128,3584]{4,3,2,1,0:T(8,128)(2,1)}, u32[]{:S(2)}) copy-start(bf16[2,1,1,128,3584]{4,3,2,1,0:T(8,128)(2,1)} %param.3) | copy-start | bytes 5505028
  4.4 1.0 copy-start.2

commit v3 on v2

--- a/solution.py
+++ b/solution.py
@@ -144,7 +144,7 @@
                 tc[s, d, mr, k, r].wait_recv()
                 spread(s, d, mr, r | bits[k], k)
 
-    ahead = 4
+    ahead = nch // 2
 
     def relay(i):
         zhc[i].wait_recv()
@@ -176,54 +176,66 @@
 
         lax.fori_loop(0, slots // unroll, group, 0)
 
-    for d in range(2):
-        for s in range(2):
+    quarter = nch // 8
+
+    def relays(g):
+        for i in range(g * quarter, (g + 1) * quarter):
+            relay(i)
+
+    def start_hidden(g):
+        for i in range(g * quarter, (g + 1) * quarter):
+            zhc[i].start()
+
+    last = len(bits) - 1
+    for s in range(2):
+        for d in range(2):
             zc[s, d].start()
-    for c in xo:
-        c.start()
-    zhc[0].start()
-    zhc[1].start()
+    xo[0].start()
+    start_hidden(0)
     for s in range(2):
         for d in range(2):
             zc[s, d].wait_recv()
             xc[s, d].start()
             spread(s, d, 0, 0, -1)
-    zhc[2].start()
-    zhc[3].start()
+            if s == 0:
+                zc[s, d].wait_send()
+        start_hidden(s + 1)
+    start_hidden(3)
     for s in range(2):
         for d in range(2):
             xc[s, d].wait_recv()
             spread(s, d, 1, 0, -1)
-    relay(0)
-    relay(1)
-    relay(2)
-    for k in range(len(bits) - 1):
+    xo[1].start()
+    relays(0)
+    for k in range(last):
         for mr in range(2):
             stage_wait(0, mr, k)
-    relay(3)
-    last = len(bits) - 1
+    relays(1)
     stage_wait(0, 0, last)
     fetch_own.wait()
     compute([(own, 0, 0), (own, 1, 0)], [(c00, 0), (c00, 1)], "first")
-    relay(4)
+    relays(2)
     stage_wait(0, 1, last)
     for c in xo:
         c.wait_recv()
     compute([(xh0, 0, 0), (xh0, 1, 0)], [(c01, 0), (c01, 1)], "add")
-    relay(5)
+    relays(3)
     for k in range(len(bits)):
         for mr in range(2):
             stage_wait(1, mr, k)
+    relays(4)
     for c in xr[:per]:
         c.wait_recv()
     mid = qstart - hstart
     compute([(zh, 0, mid), (xh1, 0, 0)], [(c10, 0), (c11, 0)], "add")
-    relay(6)
-    relay(7)
+    for g in range(5, 8):
+        relays(g)
     for c in xr[per:]:
         c.wait_recv()
     compute([(zh, 1, mid), (xh1, 1, 0)], [(c10, 1), (c11, 1)], "last")
-    for c in list(zc.values()) + xo + list(xc.values()) + list(tc.values()) + xr:
+    zc[1, 0].wait_send()
+    zc[1, 1].wait_send()
+    for c in xo + list(xc.values()) + list(tc.values()) + xr:
         c.wait_send()
 
 
@@ -245,7 +257,7 @@
     rel = jnp.clip(targets // db - pick(qs, half, m), 0, qw - 1)
     col = targets % db
     per_t = dm // BLK
-    nch = 8
+    nch = 16
     unroll = max(u for u in range(1, 10) if slots % u == 0)
     sizes = (S, T, rows, hw, qw, hs, qs, slots, nch, unroll, per_t)
     bf = jnp.bfloat16
@@ -266,7 +278,7 @@
         + [dma((4,)), dma((4,)), dma((nch,)), dma((nch,)), dma((2,)), dma((2,)), dma((nch,)), dma((nch,)),
            dma((4,)), dma((4,)), dma((n_tc,)), dma((n_tc,))],
         compiler_params=pltpu.CompilerParams(
-            collective_id=0, has_side_effects=True, vmem_limit_bytes=48 * 1024 * 1024),
+            collective_id=0, has_side_effects=True, vmem_limit_bytes=63 * 1024 * 1024),
         cost_estimate=pl.CostEstimate(
             flops=slots * BLK * BLK * rows * 16, bytes_accessed=8 * 1024 * 1024, transcendentals=0),
     )(rel.astype(jnp.int32), col.astype(jnp.int32), use,

time: 126 us -> 120 us (0.952); the launches traced: 124 us -> 120 us
  Pallas kernels: 114 us -> 111 us
  local copies, waits for them, and re-layouts: 8.91 us -> 6.38 us
    pallas_call x1, Pallas kernels: 114 us -> 111 us  [body(): pl.pallas_call(functools.partial(kernel, sizes), out_shape=jax.ShapeDtype...]
    unnamed x7 -> x3, local copies, waits for them, and re-layouts: 8.01 us -> 5.47 us
where the time goes in v3:
time: 120 us
  Pallas kernels  111 us (92%)
  local copies, waits for them, and re-layouts  6.38 us (5%)
  other arithmetic  2.39 us (2%)
    pallas_call x1, Pallas kernels, body(): pl.pallas_call(functools.partial(kernel, sizes), out_shape=jax.ShapeDtype...  111 us
    unnamed x3, local copies, waits for them, and re-layouts  5.47 us

profile of v3, /device:TPU:0, one launch (start us, length us, event | category | flops | bytes accessed | tf_op | source)
XLA Modules:
  0.0 119.9 jit_solution(1888387787972840376)
XLA Ops:
  0.0 0.0 copy-start
  0.0 0.7 copy-done
  0.7 0.1 dynamic-slice_reduce_fusion
  0.8 0.1 reshape.42
  0.9 0.3 reduce-window.9
  1.2 0.1 slice.10
  1.3 0.1 slice_reduce_fusion
  1.4 0.1 add_bitcast_fusion
  1.5 0.6 slice.12
  2.0 0.2 convert_reduce_fusion
  2.2 1.2 %compare_convert_fusion.use_ref = f32[126]{0:T(128)} fusion(s32[]{:T(128)} %bitcast.1, s32[]{:T(128)S(6)} %mul.18), kind=kLoop, calls=%fused_computation.4 | loop fusion | flops 378 | bytes 512 | tf_op jit(solution)/shard_map/convert_element_type | solution.py:255
  3.5 0.6 and_select_fusion
  4.1 111.1 %shard_map.37 = bf16[126,128,128]{2,1,0:T(8,128)(2,1)} custom-call(s32[126]{0:T(128)} %get-tuple-element.6.rel_ref, s32[126]{0:T(128)} %get-tuple-element.5.col_ref, f32[126]{0:T(128)} %compare_convert_fusion.use_ref, bf16[2,128,3584]{2,1,0:T(8,128)(2,1)} %bitcast.7, bf16[2,128,1024]{2,1,0:T(8,128)(2,1)} %bitcast.8), custom_call_target="tpu_custom_call" | custom-call | flops 4227858432 | bytes 8388608 | tf_op jit(solution)/shard_map/pallas_call | solution.py:268
  115.2 4.7 %copy.5 = bf16[1,1,126,128,128]{4,3,2,1,0:T(8,128)(2,1)} copy(bf16[1,1,126,128,128]{4,3,2,1,0:T(8,128)(2,1)} %bitcast.6) | data formatting | bytes 8257536
  (2 shorter events, 0.0 us)
Async XLA Ops:
  0.0 0.7 copy-start

commit v4 on v3

--- a/solution.py
+++ b/solution.py
@@ -52,8 +52,32 @@
     return u
 
 
-def kernel(sizes, rel_ref, col_ref, use_ref, h_ref, inc_ref, out_ref,
-           inc_b, c00, c01, c10, c11, zh, xh0, xh1, h_t, acc, inc_v, own, in_s,
+def slot_table(mask, first, qstart, qw, lanes):
+    f, db = mask.shape
+    kept = mask.astype(jnp.float32)
+
+    def iota(shape, dim):
+        return lax.broadcasted_iota(jnp.int32, shape, dim)
+
+    upper = (iota((db, db), 0) <= iota((db, db), 1)).astype(jnp.float32)
+    lower = (iota((f, f), 1) < iota((f, f), 0)).astype(jnp.float32)
+    within = jnp.dot(kept, upper, preferred_element_type=jnp.float32)
+    above = jnp.dot(lower, kept, preferred_element_type=jnp.float32)
+    before = jnp.sum(above, axis=1, keepdims=True)
+    end = before + jnp.sum(kept, axis=1, keepdims=True)
+    pos = (first + iota((1, lanes), 1)).astype(jnp.float32)
+    row = jnp.sum((end <= pos).astype(jnp.float32), axis=0, keepdims=True)
+    hot = (iota((f, lanes), 0).astype(jnp.float32) == row).astype(jnp.float32)
+    mine = pos - jnp.sum(hot * before, axis=0, keepdims=True)
+    running = lax.dot_general(within, hot, (((0,), (0,)), ((), ())), preferred_element_type=jnp.float32)
+    col = jnp.sum((running <= mine).astype(jnp.float32), axis=0, keepdims=True)
+    use = (row < f).astype(jnp.int32)
+    rel = jnp.clip(row.astype(jnp.int32) - qstart, 0, qw - 1)
+    return rel, jnp.clip(col.astype(jnp.int32), 0, db - 1), use
+
+
+def kernel(sizes, mask_ref, h_ref, inc_ref, out_ref,
+           inc_b, c00, c01, c10, c11, zh, xh0, xh1, h_t, acc, inc_v, own, in_s, tab_v, tab,
            zc_s, zc_r, zh_s, zh_r, xo_s, xo_r, xr_s, xr_r, xc_s, xc_r, tc_s, tc_r):
     S, T, rows, hw, qw, hs, qs, slots, nch, unroll, cpt = sizes
     p, t, m = lax.axis_index("section"), lax.axis_index("tp"), lax.axis_index("mirror")
@@ -145,6 +169,7 @@
                 spread(s, d, mr, r | bits[k], k)
 
     ahead = nch // 2
+    last_col = T * cpt - 1
 
     def relay(i):
         zhc[i].wait_recv()
@@ -164,12 +189,13 @@
         def group(g, carry):
             for e in range(unroll):
                 k = g * unroll + e
-                right = jnp.concatenate([ref[d, col_ref[k]] for ref, d in rights], axis=0)
-                got = jnp.dot(h_t[rel_ref[k]], right, preferred_element_type=jnp.float32)
+                rel, col = jnp.clip(tab[0, k], 0, qw - 1), jnp.clip(tab[1, k], 0, last_col)
+                right = jnp.concatenate([ref[d, col] for ref, d in rights], axis=0)
+                got = jnp.dot(h_t[rel], right, preferred_element_type=jnp.float32)
                 if kind != "first":
                     got = got + acc[k]
                 if kind == "last":
-                    out_ref[k] = (got * use_ref[k]).astype(out_ref.dtype)
+                    out_ref[k] = (got * tab[2, k].astype(jnp.float32)).astype(out_ref.dtype)
                 else:
                     acc[k] = got
             return carry
@@ -192,6 +218,13 @@
             zc[s, d].start()
     xo[0].start()
     start_hidden(0)
+    rel, col, use = slot_table(mask_ref[p % (S // 2)], (2 * half + m) * slots, qstart, qw, tab_v.shape[1])
+    tab_v[...] = jnp.zeros_like(tab_v)
+    tab_v[0:1] = rel
+    tab_v[1:2] = col
+    tab_v[2:3] = use
+    put_tab = pltpu.make_async_copy(tab_v, tab, in_s.at[2])
+    put_tab.start()
     for s in range(2):
         for d in range(2):
             zc[s, d].wait_recv()
@@ -213,6 +246,7 @@
     relays(1)
     stage_wait(0, 0, last)
     fetch_own.wait()
+    put_tab.wait()
     compute([(own, 0, 0), (own, 1, 0)], [(c00, 0), (c00, 1)], "first")
     relays(2)
     stage_wait(0, 1, last)
@@ -241,47 +275,39 @@
 
 def body(hidden, incoming, block_mask):
     S, T = lax.axis_size("section"), lax.axis_size("tp")
-    p, m = lax.axis_index("section"), lax.axis_index("mirror")
     _, ffb, db = block_mask.shape
     rows, ff, dm = hidden.shape[3], hidden.shape[4], incoming.shape[4]
     cap = ffb * db * 9 // 16
     slots = cap // 4
     hw, qw, hs, qs = windows(ffb, db)
-    half = p // (S // 2)
-    mask = lax.dynamic_index_in_dim(block_mask, p % (S // 2), 0, keepdims=False)
-    running = jnp.cumsum(mask.reshape(-1))
-    positions = (2 * half + m) * slots + jnp.arange(slots, dtype=jnp.int32)
-    targets = jnp.sum((running[None, :] <= positions[:, None]).astype(jnp.int32), axis=1)
-    use = (positions < running[-1]).astype(jnp.float32)
-    targets = jnp.minimum(targets, ffb * db - 1)
-    rel = jnp.clip(targets // db - pick(qs, half, m), 0, qw - 1)
-    col = targets % db
     per_t = dm // BLK
     nch = 16
     unroll = max(u for u in range(1, 10) if slots % u == 0)
     sizes = (S, T, rows, hw, qw, hs, qs, slots, nch, unroll, per_t)
     bf = jnp.bfloat16
-    vmem, smem = pl.BlockSpec(memory_space=pltpu.VMEM), pl.BlockSpec(memory_space=pltpu.SMEM)
+    lanes = cdiv(slots, BLK) * BLK
+    vmem = pl.BlockSpec(memory_space=pltpu.VMEM)
     hbm = pl.BlockSpec(memory_space=pltpu.HBM)
     dma = pltpu.SemaphoreType.DMA
     n_tc = 8 * (T - 1)
     out = pl.pallas_call(
         functools.partial(kernel, sizes),
         out_shape=jax.ShapeDtypeStruct((slots, BLK, BLK), bf),
-        in_specs=[smem] * 3 + [hbm] * 2,
+        in_specs=[vmem] + [hbm] * 2,
         out_specs=vmem,
         scratch_shapes=[pltpu.VMEM((2, per_t, rows, BLK), bf)] + [pltpu.VMEM((2, db, rows, BLK), bf)] * 4
         + [pltpu.VMEM((2, rows, hw * BLK), bf)]
         + [pltpu.VMEM((2, rows, qw * BLK), bf)] * 2
         + [pltpu.VMEM((qw, BLK, 2 * rows), bf), pltpu.VMEM((slots, BLK, BLK), jnp.float32)]
-        + [pltpu.VMEM((2, rows, dm), bf), pltpu.VMEM((2, rows, qw * BLK), bf), dma((2,))]
+        + [pltpu.VMEM((2, rows, dm), bf), pltpu.VMEM((2, rows, qw * BLK), bf), dma((3,)),
+           pltpu.VMEM((8, lanes), jnp.int32), pltpu.SMEM((8, lanes), jnp.int32)]
         + [dma((4,)), dma((4,)), dma((nch,)), dma((nch,)), dma((2,)), dma((2,)), dma((nch,)), dma((nch,)),
            dma((4,)), dma((4,)), dma((n_tc,)), dma((n_tc,))],
         compiler_params=pltpu.CompilerParams(
             collective_id=0, has_side_effects=True, vmem_limit_bytes=63 * 1024 * 1024),
         cost_estimate=pl.CostEstimate(
             flops=slots * BLK * BLK * rows * 16, bytes_accessed=8 * 1024 * 1024, transcendentals=0),
-    )(rel.astype(jnp.int32), col.astype(jnp.int32), use,
+    )(block_mask,
       hidden.reshape(2, rows, ff), incoming.reshape(2, rows, dm))
     return out.reshape(1, 1, slots, BLK, BLK)
 

time: 120 us -> 118 us (0.983)
  other arithmetic: 2.39 us -> 0 us
    convert_element_type x1 -> x0, other arithmetic: 1.25 us -> none  [body(): use = (positions < running[-1]).astype(jnp.float32)]
    unnamed x3 -> x2, local copies, waits for them, and re-layouts: 5.47 us -> 6.09 us
where the time goes in v4:
time: 118 us; the launch traced here: 117 us
  Pallas kernels  111 us (94%)
  local copies, waits for them, and re-layouts  6.09 us (5%)
    pallas_call x1, Pallas kernels, body(): pl.pallas_call(functools.partial(kernel, sizes), out_shape=jax.ShapeDtype...  111 us
    unnamed x2, local copies, waits for them, and re-layouts  6.09 us

profile of v4, /device:TPU:0, one launch (start us, length us, event | category | flops | bytes accessed | tf_op | source)
XLA Modules:
  0.0 117.3 jit_solution(6021295681846168189)
XLA Ops:
  0.0 1.4 %copy.4.mask_ref = s32[2,28,32]{2,1,0:T(8,128)} copy(s32[2,28,32]{2,0,1:T(2,128)} %param.5) | data formatting | bytes 14336 | tf_op args[2]
  1.4 111.2 %shard_map.37 = bf16[126,128,128]{2,1,0:T(8,128)(2,1)} custom-call(s32[2,28,32]{2,1,0:T(8,128)} %copy.4.mask_ref, bf16[2,128,3584]{2,1,0:T(8,128)(2,1)} %bitcast.4, bf16[2,128,1024]{2,1,0:T(8,128)(2,1)} %bitcast.5), custom_call_target="tpu_custom_call" | custom-call | flops 4227858432 | bytes 8388608 | tf_op jit(solution)/shard_map/pallas_call | solution.py:293
  112.6 4.7 %copy.6 = bf16[1,1,126,128,128]{4,3,2,1,0:T(8,128)(2,1)} copy(bf16[1,1,126,128,128]{4,3,2,1,0:T(8,128)(2,1)} %bitcast.3) | data formatting | bytes 8257536

commit v5 on v4

--- a/solution.py
+++ b/solution.py
@@ -31,6 +31,7 @@
         h = q // 2
         qs[q] = max(hs[h], min(qs[q], hs[h] + hw - qw))
         assert qs[q] <= quarters[q][0] and qs[q] + qw > quarters[q][1]
+        assert qs[q] - hs[h] in (0, hw - qw)
         assert hs[h] <= halves[h][0] and hs[h] + hw > halves[h][1]
     return hw, qw, hs, qs
 
@@ -127,13 +128,25 @@
             zc[s, d] = copy(inc_b.at[d], C[s][0].at[d, mine], zc_s.at[i], zc_r.at[i], {"section": dest})
     per = nch // 2
     step = rows // per
-    zhc, xr = [], []
+    zhc, xr, relay_of = [], [], {}
+    qstart_cross = pick(qs, 1 - half, other)
+    spare = max(hw - qw, 1)
+
+    def rest(start, base):
+        return qw * (1 - (start - base) // spare)
+
     for i in range(nch):
         d, r = i // per, pl.ds((i % per) * step, step)
-        zhc.append(copy(h_ref.at[d, r, cols(hstart_there, hw)], zh.at[d, r], zh_s.at[i], zh_r.at[i],
-                        {"section": partner}))
+        zhc.append(copy(h_ref.at[d, r, cols(qstart_cross, qw)], zh.at[d, r, cols(qstart_cross - hstart_there, qw)],
+                        zh_s.at[len(zhc)], zh_r.at[len(zhc)], {"section": partner}))
         xr.append(copy(zh.at[d, r, cols(qstart_there - hstart, qw)], xh1.at[d, r], xr_s.at[i], xr_r.at[i],
                        {"mirror": other}))
+        relay_of[len(zhc) - 1] = xr[-1]
+        if i % per == per - 1 and hw > qw:
+            away = rest(qstart_cross, hstart_there)
+            zhc.append(copy(h_ref.at[d, :, cols(hstart_there + away, hw - qw)], zh.at[d, :, cols(away, hw - qw)],
+                            zh_s.at[len(zhc)], zh_r.at[len(zhc)], {"section": partner}))
+    items = len(zhc)
     xo = [copy(h_ref.at[d, :, cols(qstart_there, qw)], xh0.at[d], xo_s.at[d], xo_r.at[d], {"mirror": other})
           for d in range(2)]
     xc = {}
@@ -173,9 +186,10 @@
 
     def relay(i):
         zhc[i].wait_recv()
-        xr[i].start()
+        if i in relay_of:
+            relay_of[i].start()
         zhc[i].wait_send()
-        if i + ahead < nch:
+        if i + ahead < items:
             zhc[i + ahead].start()
 
     def compute(lefts, rights, kind):
@@ -203,10 +217,13 @@
         lax.fori_loop(0, slots // unroll, group, 0)
 
     quarter = nch // 8
-
-    def relays(g):
-        for i in range(g * quarter, (g + 1) * quarter):
+    done = [0]
+    half_items = items // 2
+
+    def relays(upto):
+        for i in range(done[0], upto):
             relay(i)
+        done[0] = upto
 
     def start_hidden(g):
         for i in range(g * quarter, (g + 1) * quarter):
@@ -218,7 +235,7 @@
             zc[s, d].start()
     xo[0].start()
     start_hidden(0)
-    rel, col, use = slot_table(mask_ref[p % (S // 2)], (2 * half + m) * slots, qstart, qw, tab_v.shape[1])
+    rel, col, use = slot_table(mask_ref[:, p % (S // 2)], (2 * half + m) * slots, qstart, qw, tab_v.shape[1])
     tab_v[...] = jnp.zeros_like(tab_v)
     tab_v[0:1] = rel
     tab_v[1:2] = col
@@ -239,31 +256,30 @@
             xc[s, d].wait_recv()
             spread(s, d, 1, 0, -1)
     xo[1].start()
-    relays(0)
+    relays(quarter)
     for k in range(last):
         for mr in range(2):
             stage_wait(0, mr, k)
-    relays(1)
+    relays(2 * quarter)
     stage_wait(0, 0, last)
     fetch_own.wait()
     put_tab.wait()
     compute([(own, 0, 0), (own, 1, 0)], [(c00, 0), (c00, 1)], "first")
-    relays(2)
+    relays(3 * quarter)
     stage_wait(0, 1, last)
     for c in xo:
         c.wait_recv()
     compute([(xh0, 0, 0), (xh0, 1, 0)], [(c01, 0), (c01, 1)], "add")
-    relays(3)
+    relays(half_items)
     for k in range(len(bits)):
         for mr in range(2):
             stage_wait(1, mr, k)
-    relays(4)
+    relays(half_items + quarter)
     for c in xr[:per]:
         c.wait_recv()
     mid = qstart - hstart
     compute([(zh, 0, mid), (xh1, 0, 0)], [(c10, 0), (c11, 0)], "add")
-    for g in range(5, 8):
-        relays(g)
+    relays(items)
     for c in xr[per:]:
         c.wait_recv()
     compute([(zh, 1, mid), (xh1, 1, 0)], [(c10, 1), (c11, 1)], "last")
@@ -282,7 +298,7 @@
     hw, qw, hs, qs = windows(ffb, db)
     per_t = dm // BLK
     nch = 16
-    unroll = max(u for u in range(1, 10) if slots % u == 0)
+    unroll = max(u for u in range(1, 22) if slots % u == 0)
     sizes = (S, T, rows, hw, qw, hs, qs, slots, nch, unroll, per_t)
     bf = jnp.bfloat16
     lanes = cdiv(slots, BLK) * BLK
@@ -301,13 +317,13 @@
         + [pltpu.VMEM((qw, BLK, 2 * rows), bf), pltpu.VMEM((slots, BLK, BLK), jnp.float32)]
         + [pltpu.VMEM((2, rows, dm), bf), pltpu.VMEM((2, rows, qw * BLK), bf), dma((3,)),
            pltpu.VMEM((8, lanes), jnp.int32), pltpu.SMEM((8, lanes), jnp.int32)]
-        + [dma((4,)), dma((4,)), dma((nch,)), dma((nch,)), dma((2,)), dma((2,)), dma((nch,)), dma((nch,)),
+        + [dma((4,)), dma((4,)), dma((nch + 2,)), dma((nch + 2,)), dma((2,)), dma((2,)), dma((nch,)), dma((nch,)),
            dma((4,)), dma((4,)), dma((n_tc,)), dma((n_tc,))],
         compiler_params=pltpu.CompilerParams(
             collective_id=0, has_side_effects=True, vmem_limit_bytes=63 * 1024 * 1024),
         cost_estimate=pl.CostEstimate(
             flops=slots * BLK * BLK * rows * 16, bytes_accessed=8 * 1024 * 1024, transcendentals=0),
-    )(block_mask,
+    )(jnp.transpose(block_mask, (1, 0, 2)),
       hidden.reshape(2, rows, ff), incoming.reshape(2, rows, dm))
     return out.reshape(1, 1, slots, BLK, BLK)
 

time: 118 us -> 112 us (0.949)
  Pallas kernels: 111 us -> 107 us
  local copies, waits for them, and re-layouts: 6.09 us -> 4.73 us
    pallas_call x1, Pallas kernels: 111 us -> 107 us  [body(): pl.pallas_call(functools.partial(kernel, sizes), out_shape=jax.ShapeDtype...]
    unnamed x2 -> x1, local copies, waits for them, and re-layouts: 6.09 us -> 4.73 us
where the time goes in v5:
time: 112 us
  Pallas kernels  107 us (96%)
  local copies, waits for them, and re-layouts  4.73 us (4%)
    pallas_call x1, Pallas kernels, body(): pl.pallas_call(functools.partial(kernel, sizes), out_shape=jax.ShapeDtype...  107 us
    unnamed x1, local copies, waits for them, and re-layouts  4.73 us

profile of v5, /device:TPU:0, one launch (start us, length us, event | category | flops | bytes accessed | tf_op | source)
XLA Modules:
  0.0 112.2 jit_solution(15705493512274636096)
XLA Ops:
  0.0 107.5 %shard_map.37 = bf16[126,128,128]{2,1,0:T(8,128)(2,1)} custom-call(s32[28,2,32]{2,1,0:T(2,128)} %bitcast.7, bf16[2,128,3584]{2,1,0:T(8,128)(2,1)} %bitcast.5, bf16[2,128,1024]{2,1,0:T(8,128)(2,1)} %bitcast.6), custom_call_target="tpu_custom_call" | custom-call | flops 4227858432 | bytes 8388608 | tf_op jit(solution)/shard_map/pallas_call | solution.py:309
  107.5 4.7 %copy.5 = bf16[1,1,126,128,128]{4,3,2,1,0:T(8,128)(2,1)} copy(bf16[1,1,126,128,128]{4,3,2,1,0:T(8,128)(2,1)} %bitcast.4) | data formatting | bytes 8257536

commit v6 on v5

--- a/solution.py
+++ b/solution.py
@@ -77,8 +77,8 @@
     return rel, jnp.clip(col.astype(jnp.int32), 0, db - 1), use
 
 
-def kernel(sizes, mask_ref, h_ref, inc_ref, out_ref,
-           inc_b, c00, c01, c10, c11, zh, xh0, xh1, h_t, acc, inc_v, own, in_s, tab_v, tab,
+def kernel(sizes, mask_ref, h_ref, inc_ref, acc_out, cot_out, turned_out, tab_out,
+           inc_b, c00, c01, c10, c11, zh, xh0, xh1, h_t, acc, inc_v, own, in_s, tab_v, tab, out_s,
            zc_s, zc_r, zh_s, zh_r, xo_s, xo_r, xr_s, xr_r, xc_s, xc_r, tc_s, tc_r):
     S, T, rows, hw, qw, hs, qs, slots, nch, unroll, cpt = sizes
     p, t, m = lax.axis_index("section"), lax.axis_index("tp"), lax.axis_index("mirror")
@@ -110,10 +110,6 @@
     fetch_own = pltpu.make_async_copy(h_ref.at[:, :, cols(qstart, qw)], own, in_s.at[1])
     fetch_inc.start()
     fetch_own.start()
-    fetch_inc.wait()
-    for d in range(2):
-        for c in range(cpt):
-            inc_b[d, c] = inc_v[d, :, c * BLK:(c + 1) * BLK]
     pl.semaphore_wait(barrier, len(peers))
 
     def copy(src, dst, ss, rs, dev):
@@ -192,13 +188,16 @@
         if i + ahead < items:
             zhc[i + ahead].start()
 
-    def compute(lefts, rights, kind):
+    def turn_all(lefts):
         def turn(b, carry):
             blk = jnp.concatenate([ref[d, :, cols(first + b, 1)] for ref, d, first in lefts], axis=0)
             h_t[b] = blk.T
             return carry
 
         lax.fori_loop(0, qw, turn, 0)
+
+    def compute(lefts, rights, kind):
+        turn_all(lefts)
 
         def group(g, carry):
             for e in range(unroll):
@@ -208,10 +207,7 @@
                 got = jnp.dot(h_t[rel], right, preferred_element_type=jnp.float32)
                 if kind != "first":
                     got = got + acc[k]
-                if kind == "last":
-                    out_ref[k] = (got * tab[2, k].astype(jnp.float32)).astype(out_ref.dtype)
-                else:
-                    acc[k] = got
+                acc[k] = got
             return carry
 
         lax.fori_loop(0, slots // unroll, group, 0)
@@ -230,11 +226,17 @@
             zhc[i].start()
 
     last = len(bits) - 1
+    zhc[0].start()
+    xo[0].start()
+    fetch_inc.wait()
+    for d in range(2):
+        for c in range(cpt):
+            inc_b[d, c] = inc_v[d, :, c * BLK:(c + 1) * BLK]
     for s in range(2):
         for d in range(2):
             zc[s, d].start()
-    xo[0].start()
-    start_hidden(0)
+    for i in range(1, quarter):
+        zhc[i].start()
     rel, col, use = slot_table(mask_ref[:, p % (S // 2)], (2 * half + m) * slots, qstart, qw, tab_v.shape[1])
     tab_v[...] = jnp.zeros_like(tab_v)
     tab_v[0:1] = rel
@@ -279,14 +281,32 @@
         c.wait_recv()
     mid = qstart - hstart
     compute([(zh, 0, mid), (xh1, 0, 0)], [(c10, 0), (c11, 0)], "add")
+    keep = [pltpu.make_async_copy(src, dst, out_s.at[i]) for i, (src, dst) in enumerate((
+        (acc, acc_out), (c10.at[1], cot_out.at[0]), (c11.at[1], cot_out.at[1]), (tab_v, tab_out), (h_t, turned_out)))]
+    for c in keep[:-1]:
+        c.start()
     relays(items)
     for c in xr[per:]:
         c.wait_recv()
-    compute([(zh, 1, mid), (xh1, 1, 0)], [(c10, 1), (c11, 1)], "last")
+    turn_all([(zh, 1, mid), (xh1, 1, 0)])
+    keep[-1].start()
+    for c in keep:
+        c.wait()
     zc[1, 0].wait_send()
     zc[1, 1].wait_send()
     for c in xo + list(xc.values()) + list(tc.values()) + xr:
         c.wait_send()
+
+
+def last_pass(unroll, tab, turned, cot, acc, out):
+    base = pl.program_id(0) * unroll
+    qw, last_col = turned.shape[0], cot.shape[1] - 1
+    for e in range(unroll):
+        k = base + e
+        rel, col = jnp.clip(tab[0, k], 0, qw - 1), jnp.clip(tab[1, k], 0, last_col)
+        right = jnp.concatenate([cot[0, col], cot[1, col]], axis=0)
+        got = acc[e] + jnp.dot(turned[rel], right, preferred_element_type=jnp.float32)
+        out[e] = (got * tab[2, k].astype(jnp.float32)).astype(out.dtype)
 
 
 def body(hidden, incoming, block_mask):
@@ -306,25 +326,41 @@
     hbm = pl.BlockSpec(memory_space=pltpu.HBM)
     dma = pltpu.SemaphoreType.DMA
     n_tc = 8 * (T - 1)
-    out = pl.pallas_call(
+    acc, cot, turned, tab = pl.pallas_call(
         functools.partial(kernel, sizes),
-        out_shape=jax.ShapeDtypeStruct((slots, BLK, BLK), bf),
+        out_shape=[
+            jax.ShapeDtypeStruct((slots, BLK, BLK), jnp.float32),
+            jax.ShapeDtypeStruct((2, db, rows, BLK), bf),
+            jax.ShapeDtypeStruct((qw, BLK, 2 * rows), bf),
+            jax.ShapeDtypeStruct((8, lanes), jnp.int32),
+        ],
         in_specs=[vmem] + [hbm] * 2,
-        out_specs=vmem,
+        out_specs=[hbm] * 4,
         scratch_shapes=[pltpu.VMEM((2, per_t, rows, BLK), bf)] + [pltpu.VMEM((2, db, rows, BLK), bf)] * 4
         + [pltpu.VMEM((2, rows, hw * BLK), bf)]
         + [pltpu.VMEM((2, rows, qw * BLK), bf)] * 2
         + [pltpu.VMEM((qw, BLK, 2 * rows), bf), pltpu.VMEM((slots, BLK, BLK), jnp.float32)]
         + [pltpu.VMEM((2, rows, dm), bf), pltpu.VMEM((2, rows, qw * BLK), bf), dma((3,)),
-           pltpu.VMEM((8, lanes), jnp.int32), pltpu.SMEM((8, lanes), jnp.int32)]
+           pltpu.VMEM((8, lanes), jnp.int32), pltpu.SMEM((8, lanes), jnp.int32), dma((5,))]
         + [dma((4,)), dma((4,)), dma((nch + 2,)), dma((nch + 2,)), dma((2,)), dma((2,)), dma((nch,)), dma((nch,)),
            dma((4,)), dma((4,)), dma((n_tc,)), dma((n_tc,))],
         compiler_params=pltpu.CompilerParams(
             collective_id=0, has_side_effects=True, vmem_limit_bytes=63 * 1024 * 1024),
         cost_estimate=pl.CostEstimate(
-            flops=slots * BLK * BLK * rows * 16, bytes_accessed=8 * 1024 * 1024, transcendentals=0),
+            flops=slots * BLK * BLK * rows * 12, bytes_accessed=16 * 1024 * 1024, transcendentals=0),
     )(jnp.transpose(block_mask, (1, 0, 2)),
       hidden.reshape(2, rows, ff), incoming.reshape(2, rows, dm))
+    per_step = pl.BlockSpec((unroll, BLK, BLK), lambda g: (g, 0, 0))
+    out = pl.pallas_call(
+        functools.partial(last_pass, unroll),
+        grid=(slots // unroll,),
+        out_shape=jax.ShapeDtypeStruct((slots, BLK, BLK), bf),
+        in_specs=[pl.BlockSpec(memory_space=pltpu.SMEM), vmem, vmem, per_step],
+        out_specs=per_step,
+        compiler_params=pltpu.CompilerParams(vmem_limit_bytes=63 * 1024 * 1024),
+        cost_estimate=pl.CostEstimate(
+            flops=slots * BLK * BLK * rows * 4, bytes_accessed=16 * 1024 * 1024, transcendentals=0),
+    )(tab, turned, cot, acc)
     return out.reshape(1, 1, slots, BLK, BLK)
 
 

time: 112 us -> 113 us (level)
  Pallas kernels: 107 us -> 113 us
  local copies, waits for them, and re-layouts: 4.73 us -> 0 us
    pallas_call x1 -> x2, Pallas kernels: 107 us -> 113 us  [the longest x1 104 us: body(): pl.pallas_call(functools.partial(kernel, sizes), out_shape=[jax.ShapeDtyp...]
    unnamed x1 -> x0, local copies, waits for them, and re-layouts: 4.73 us -> none
where the time goes in v6:
time: 113 us
  Pallas kernels  113 us (100%)
    pallas_call x1, Pallas kernels, body(): pl.pallas_call(functools.partial(kernel, sizes), out_shape=[jax.ShapeDtyp...  104 us
    pallas_call x1, Pallas kernels, body(): pl.pallas_call(functools.partial(last_pass, unroll), grid=(slots // unrol...  9.17 us

profile of v6, /device:TPU:0, one launch (start us, length us, event | category | flops | bytes accessed | tf_op | source)
XLA Modules:
  0.0 112.9 jit_solution(4193393115219882111)
XLA Ops:
  0.0 103.7 %shard_map.37 = (f32[126,128,128]{2,1,0:T(8,128)}, bf16[2,32,128,128]{3,2,1,0:T(8,128)(2,1)}, bf16[21,128,256]{2,1,0:T(8,128)(2,1)}, s32[8,128]{1,0:T(8,128)}) custom-call(s32[28,2,32]{2,1,0:T(2,128)} %bitcast.6, bf16[2,128,3584]{2,1,0:T(8,128)(2,1)} %bitcast.4, bf16[2,128,1024]{2,1,0:T(8,128)(2,1)} %bitcast.5), custom_call_target="tpu_custom_call" | custom-call | flops 3170893824 | bytes 16777216 | tf_op jit(solution)/shard_map/pallas_call | solution.py:329
  103.7 9.2 %shard_map.38 = bf16[126,128,128]{2,1,0:T(8,128)(2,1)} custom-call(s32[8,128]{1,0:T(8,128)} %get-tuple-element.9.tab, bf16[21,128,256]{2,1,0:T(8,128)(2,1)} %get-tuple-element.10.turned, bf16[2,32,128,128]{3,2,1,0:T(8,128)(2,1)} %get-tuple-element.11.cot, f32[126,128,128]{2,1,0:T(8,128)} %get-tuple-element.12.acc), custom_call_target="tpu_custom_call" | custom-call | flops 1056964608 | bytes 16777216 | tf_op jit(solution)/shard_map/pallas_call | solution.py:354

commit v7 on v5

--- a/solution.py
+++ b/solution.py
@@ -78,7 +78,7 @@
 
 
 def kernel(sizes, mask_ref, h_ref, inc_ref, out_ref,
-           inc_b, c00, c01, c10, c11, zh, xh0, xh1, h_t, acc, inc_v, own, in_s, tab_v, tab,
+           inc_b, c00, c01, c10, c11, zh, xh0, xh1, h_t, acc, inc_v, own, in_s, tab_v, tab, out_v, out_s,
            zc_s, zc_r, zh_s, zh_r, xo_s, xo_r, xr_s, xr_r, xc_s, xc_r, tc_s, tc_r):
     S, T, rows, hw, qw, hs, qs, slots, nch, unroll, cpt = sizes
     p, t, m = lax.axis_index("section"), lax.axis_index("tp"), lax.axis_index("mirror")
@@ -110,10 +110,6 @@
     fetch_own = pltpu.make_async_copy(h_ref.at[:, :, cols(qstart, qw)], own, in_s.at[1])
     fetch_inc.start()
     fetch_own.start()
-    fetch_inc.wait()
-    for d in range(2):
-        for c in range(cpt):
-            inc_b[d, c] = inc_v[d, :, c * BLK:(c + 1) * BLK]
     pl.semaphore_wait(barrier, len(peers))
 
     def copy(src, dst, ss, rs, dev):
@@ -192,6 +188,10 @@
         if i + ahead < items:
             zhc[i + ahead].start()
 
+    def put(g):
+        part = pl.ds(g * unroll, unroll)
+        return pltpu.make_async_copy(out_v.at[part], out_ref.at[part], out_s.at[g])
+
     def compute(lefts, rights, kind):
         def turn(b, carry):
             blk = jnp.concatenate([ref[d, :, cols(first + b, 1)] for ref, d, first in lefts], axis=0)
@@ -209,9 +209,11 @@
                 if kind != "first":
                     got = got + acc[k]
                 if kind == "last":
-                    out_ref[k] = (got * tab[2, k].astype(jnp.float32)).astype(out_ref.dtype)
+                    out_v[k] = (got * tab[2, k].astype(jnp.float32)).astype(out_v.dtype)
                 else:
                     acc[k] = got
+            if kind == "last":
+                put(g).start()
             return carry
 
         lax.fori_loop(0, slots // unroll, group, 0)
@@ -230,11 +232,17 @@
             zhc[i].start()
 
     last = len(bits) - 1
+    zhc[0].start()
+    xo[0].start()
+    fetch_inc.wait()
+    for d in range(2):
+        for c in range(cpt):
+            inc_b[d, c] = inc_v[d, :, c * BLK:(c + 1) * BLK]
     for s in range(2):
         for d in range(2):
             zc[s, d].start()
-    xo[0].start()
-    start_hidden(0)
+    for i in range(1, quarter):
+        zhc[i].start()
     rel, col, use = slot_table(mask_ref[:, p % (S // 2)], (2 * half + m) * slots, qstart, qw, tab_v.shape[1])
     tab_v[...] = jnp.zeros_like(tab_v)
     tab_v[0:1] = rel
@@ -283,10 +291,16 @@
     for c in xr[per:]:
         c.wait_recv()
     compute([(zh, 1, mid), (xh1, 1, 0)], [(c10, 1), (c11, 1)], "last")
+    for g in range(slots // unroll):
+        put(g).wait()
     zc[1, 0].wait_send()
     zc[1, 1].wait_send()
     for c in xo + list(xc.values()) + list(tc.values()) + xr:
         c.wait_send()
+
+
+def hand_over(src, dst):
+    dst[...] = src[...]
 
 
 def body(hidden, incoming, block_mask):
@@ -310,13 +324,14 @@
         functools.partial(kernel, sizes),
         out_shape=jax.ShapeDtypeStruct((slots, BLK, BLK), bf),
         in_specs=[vmem] + [hbm] * 2,
-        out_specs=vmem,
+        out_specs=hbm,
         scratch_shapes=[pltpu.VMEM((2, per_t, rows, BLK), bf)] + [pltpu.VMEM((2, db, rows, BLK), bf)] * 4
         + [pltpu.VMEM((2, rows, hw * BLK), bf)]
         + [pltpu.VMEM((2, rows, qw * BLK), bf)] * 2
         + [pltpu.VMEM((qw, BLK, 2 * rows), bf), pltpu.VMEM((slots, BLK, BLK), jnp.float32)]
         + [pltpu.VMEM((2, rows, dm), bf), pltpu.VMEM((2, rows, qw * BLK), bf), dma((3,)),
-           pltpu.VMEM((8, lanes), jnp.int32), pltpu.SMEM((8, lanes), jnp.int32)]
+           pltpu.VMEM((8, lanes), jnp.int32), pltpu.SMEM((8, lanes), jnp.int32),
+           pltpu.VMEM((slots, BLK, BLK), bf), dma((slots // unroll,))]
         + [dma((4,)), dma((4,)), dma((nch + 2,)), dma((nch + 2,)), dma((2,)), dma((2,)), dma((nch,)), dma((nch,)),
            dma((4,)), dma((4,)), dma((n_tc,)), dma((n_tc,))],
         compiler_params=pltpu.CompilerParams(
@@ -325,6 +340,15 @@
             flops=slots * BLK * BLK * rows * 16, bytes_accessed=8 * 1024 * 1024, transcendentals=0),
     )(jnp.transpose(block_mask, (1, 0, 2)),
       hidden.reshape(2, rows, ff), incoming.reshape(2, rows, dm))
+    part = pl.BlockSpec((unroll, BLK, BLK), lambda g: (g, 0, 0))
+    out = pl.pallas_call(
+        hand_over,
+        grid=(slots // unroll,),
+        out_shape=jax.ShapeDtypeStruct((slots, BLK, BLK), bf),
+        in_specs=[part],
+        out_specs=part,
+        compiler_params=pltpu.CompilerParams(vmem_limit_bytes=63 * 1024 * 1024),
+    )(out)
     return out.reshape(1, 1, slots, BLK, BLK)
 
 

time: 112 us -> 113 us (level)
  Pallas kernels: 107 us -> 112 us
  local copies, waits for them, and re-layouts: 4.73 us -> 0 us
    pallas_call x0 -> x1, Pallas kernels: none -> 5.73 us  [body(): pl.pallas_call(hand_over, grid=(slots // unroll,), out_shape=jax.ShapeDty...]
    unnamed x1 -> x0, local copies, waits for them, and re-layouts: 4.73 us -> none
where the time goes in v7:
time: 113 us; the launch traced here: 112 us
  Pallas kernels  112 us (99%)
    pallas_call x1, Pallas kernels, body(): pl.pallas_call(functools.partial(kernel, sizes), out_shape=jax.ShapeDtype...  107 us
    pallas_call x1, Pallas kernels, body(): pl.pallas_call(hand_over, grid=(slots // unroll,), out_shape=jax.ShapeDty...  5.73 us

profile of v7, /device:TPU:0, one launch (start us, length us, event | category | flops | bytes accessed | tf_op | source)
XLA Modules:
  0.0 112.4 jit_solution(13432456794314417948)
XLA Ops:
  0.0 106.7 %shard_map.37.src = bf16[126,128,128]{2,1,0:T(8,128)(2,1)} custom-call(s32[28,2,32]{2,1,0:T(2,128)} %bitcast.6, bf16[2,128,3584]{2,1,0:T(8,128)(2,1)} %bitcast.4, bf16[2,128,1024]{2,1,0:T(8,128)(2,1)} %bitcast.5), custom_call_target="tpu_custom_call" | custom-call | flops 4227858432 | bytes 8388608 | tf_op jit(solution)/shard_map/pallas_call | solution.py:323
  106.7 5.7 %shard_map.38 = bf16[126,128,128]{2,1,0:T(8,128)(2,1)} custom-call(bf16[126,128,128]{2,1,0:T(8,128)(2,1)} %shard_map.37.src), custom_call_target="tpu_custom_call" | custom-call | tf_op jit(solution)/shard_map/pallas_call | solution.py:344

commit v8 on v6

--- a/solution.py
+++ b/solution.py
@@ -345,7 +345,7 @@
         + [dma((4,)), dma((4,)), dma((nch + 2,)), dma((nch + 2,)), dma((2,)), dma((2,)), dma((nch,)), dma((nch,)),
            dma((4,)), dma((4,)), dma((n_tc,)), dma((n_tc,))],
         compiler_params=pltpu.CompilerParams(
-            collective_id=0, has_side_effects=True, vmem_limit_bytes=63 * 1024 * 1024),
+            collective_id=0, has_side_effects=True, vmem_limit_bytes=40 * 1024 * 1024),
         cost_estimate=pl.CostEstimate(
             flops=slots * BLK * BLK * rows * 12, bytes_accessed=16 * 1024 * 1024, transcendentals=0),
     )(jnp.transpose(block_mask, (1, 0, 2)),
@@ -357,7 +357,7 @@
         out_shape=jax.ShapeDtypeStruct((slots, BLK, BLK), bf),
         in_specs=[pl.BlockSpec(memory_space=pltpu.SMEM), vmem, vmem, per_step],
         out_specs=per_step,
-        compiler_params=pltpu.CompilerParams(vmem_limit_bytes=63 * 1024 * 1024),
+        compiler_params=pltpu.CompilerParams(vmem_limit_bytes=32 * 1024 * 1024),
         cost_estimate=pl.CostEstimate(
             flops=slots * BLK * BLK * rows * 4, bytes_accessed=16 * 1024 * 1024, transcendentals=0),
     )(tab, turned, cot, acc)

time: 113 us -> 112 us (level)
  Pallas kernels: 113 us -> 108 us
  local copies, waits for them, and re-layouts: 0 us -> 3.29 us
    pallas_call x1, Pallas kernels: 9.17 us -> 5.43 us  [body(): pl.pallas_call(functools.partial(last_pass, unroll), grid=(slots // unrol...]
    unnamed x0 -> x6, local copies, waits for them, and re-layouts: none -> 3.29 us
where the time goes in v8:
time: 112 us
  Pallas kernels  108 us (96%)
  local copies, waits for them, and re-layouts  3.29 us (3%)
    pallas_call x1, Pallas kernels, body(): pl.pallas_call(functools.partial(kernel, sizes), out_shape=[jax.ShapeDtyp...  103 us
    pallas_call x1, Pallas kernels, body(): pl.pallas_call(functools.partial(last_pass, unroll), grid=(slots // unrol...  5.43 us
    unnamed x6, local copies, waits for them, and re-layouts  3.29 us

profile of v8, /device:TPU:0, one launch (start us, length us, event | category | flops | bytes accessed | tf_op | source)
XLA Modules:
  0.0 111.6 jit_solution(18383508619611845456)
XLA Ops:
  0.0 0.0 copy-start
  0.0 1.5 %copy-done = bf16[2,1,1,128,3584]{4,3,2,1,0:T(8,128)(2,1)S(1)} copy-done((bf16[2,1,1,128,3584]{4,3,2,1,0:T(8,128)(2,1)S(1)}, bf16[2,1,1,128,3584]{4,3,2,1,0:T(8,128)(2,1)}, u32[]{:S(2)}) %copy-start) | copy-done | bytes 1835032
  1.5 0.0 copy-start.1
  1.5 1.0 copy-done.1
  2.5 0.0 copy-start.2
  2.5 0.7 copy-done.2
  3.3 102.8 %shard_map.37 = (f32[126,128,128]{2,1,0:T(8,128)S(1)}, bf16[2,32,128,128]{3,2,1,0:T(8,128)(2,1)S(1)}, bf16[21,128,256]{2,1,0:T(8,128)(2,1)S(1)}, s32[8,128]{1,0:T(8,128)S(1)}) custom-call(s32[28,2,32]{2,1,0:T(2,128)S(1)} %bitcast.6, bf16[2,128,3584]{2,1,0:T(8,128)(2,1)S(1)} %bitcast.4, bf16[2,128,1024]{2,1,0:T(8,128)(2,1)S(1)} %bitcast.5), custom_call_target="tpu_custom_call" | custom-call | flops 3170893824 | bytes 16777216 | tf_op jit(solution)/shard_map/pallas_call | solution.py:329
  106.1 5.4 %shard_map.38 = bf16[126,128,128]{2,1,0:T(8,128)(2,1)} custom-call(s32[8,128]{1,0:T(8,128)S(1)} %get-tuple-element.9.tab, bf16[21,128,256]{2,1,0:T(8,128)(2,1)S(1)} %get-tuple-element.10.turned, bf16[2,32,128,128]{3,2,1,0:T(8,128)(2,1)S(1)} %get-tuple-element.11.cot, f32[126,128,128]{2,1,0:T(8,128)S(1)} %get-tuple-element.12.acc), custom_call_target="tpu_custom_call" | custom-call | flops 1056964608 | bytes 16777216 | tf_op jit(solution)/shard_map/pallas_call | solution.py:354
Async XLA Ops:
  0.0 1.5 %copy-start = (bf16[2,1,1,128,3584]{4,3,2,1,0:T(8,128)(2,1)S(1)}, bf16[2,1,1,128,3584]{4,3,2,1,0:T(8,128)(2,1)}, u32[]{:S(2)}) copy-start(bf16[2,1,1,128,3584]{4,3,2,1,0:T(8,128)(2,1)} %param.3) | copy-start | bytes 5505028
  1.5 1.0 copy-start.1
  2.5 0.7 copy-start.2
